TPU v7x, 512 devices: a whole 4x4x16 slice. The times are simulated.
512 devices in a mesh: tm: 8 (over z_lo), rows: 64 (over z_hi, y, x, core).
Axes of the slice: x: 4, y: 4, z: 16 (z_hi: 2, z_lo: 8; z = z_hi * 8 + z_lo), core: 2. Of those that a mesh axis runs over, the one named last changes fastest.
Arguments:
- frames_in: bfloat16 [64, 128, 32, 192], P('tm', 'rows'), may hold values from -6 to 6
- slot_frame: int32 [64], P('tm'), may hold values from 0 to 63, as said below
- shot_spans: int32 [4], replicated, may hold values from 1 to 8, 16 in all
- gain_one: float32 [192], replicated, may hold values from 0.5 to 1.5
- conv_one: bfloat16 [3, 3, 3, 192, 192], replicated, may hold values from -0.078125 to 0.078125
- bias_one: float32 [192], replicated, may hold values from -3 to 3
- gain_two: float32 [192], replicated, may hold values from 0.5 to 1.5
- conv_two: bfloat16 [3, 3, 3, 192, 192], replicated, may hold values from -0.078125 to 0.078125
- bias_two: float32 [192], replicated, may hold values from -3 to 3
Outputs:
- encoded: bfloat16 [64, 128, 32, 192], P('tm', 'rows')
Inputs may be any that keep to these rules, and one draw needn't show every extreme that they name: `slot_frame`: every frame 0 to 63 is held by exactly one slot; a device's 8 slots hold, for each destination device (frame // 8), either none or exactly 2 of its frames. `shot_spans`: the counts sum to 16; the largest is 8.
All inputs are finite; a program needn't handle non-finite values.
Results may differ from a plain program's by a relative error of at most 0.0035.
Values may be sent and summed in bfloat16 or wider, within the bound.
A program may use at most 64 MiB of HBM per device.

v0:
```python
import jax
import jax.numpy as jnp
from jax import lax
from jax.sharding import PartitionSpec as P

SPAN = 4
CAP = 2


def extended_2(cells, sides, width):
    for axis, dim in sides:
        count = lax.axis_size(axis)
        ends = count - 1
        head = lax.slice_in_dim(cells, 0, width, axis=dim)
        tail = lax.slice_in_dim(cells, cells.shape[dim] - width, cells.shape[dim], axis=dim)
        cells = jnp.concatenate(
            [
                lax.ppermute(tail, axis, [(i, (i + 1) % count) for i in range(ends)]),
                cells,
                lax.ppermute(head, axis, [((i + 1) % count, i) for i in range(ends)]),
            ],
            axis=dim,
        )
    return cells


def shifted_2(block, axis, distance):
    devices = range(lax.axis_size(axis))
    route = [(i - distance, i) for i in devices if i - distance in devices]
    return lax.ppermute(block, axis, route)


def norm_silu(values, gain):
    values = values.astype(jnp.float32)
    scaled = values * lax.rsqrt(jnp.mean(values * values, axis=-1, keepdims=True) + 1e-06) * gain
    return jax.nn.silu(scaled)


def row_rims(frames_all):
    return extended_2(frames_all, (("rows", 1),), 1)


def causal_conv(extended, weight, bias_term, opened, frame_count):
    length = extended.shape[0] - 2
    row_count = extended.shape[1] - 2
    col_count = extended.shape[2]
    chan_count = extended.shape[3]
    position = jnp.arange(length) - (length - frame_count)
    within = jnp.maximum(position, 0)
    started = jnp.take(opened, within // SPAN)
    padded = jnp.pad(extended, ((0, 0), (0, 0), (1, 1), (0, 0)))
    summed = jnp.zeros((length * row_count * col_count, chan_count), jnp.float32)
    for time_tap in range(3):
        delay = 2 - time_tap
        kept_mask = (position < 0) | (within % SPAN >= delay) | jnp.logical_not(started)
        shifted = jnp.where(
            kept_mask[:, None, None, None],
            padded[time_tap : time_tap + length],
            jnp.zeros((), extended.dtype),
        )
        for row_tap in range(3):
            row_band = shifted[:, row_tap : row_tap + row_count]
            stacked = jnp.concatenate(
                [row_band[:, :, col_tap : col_tap + col_count] for col_tap in range(3)], axis=-1
            )
            stacked = stacked.reshape(-1, 3 * chan_count)
            kernel = weight[time_tap, row_tap].reshape(3 * chan_count, chan_count)
            summed = summed + jnp.dot(stacked, kernel, preferred_element_type=jnp.float32)
    return summed.reshape(length, row_count, col_count, chan_count) + bias_term


def body(
    frames_in, slot_frame, shot_spans, gain_one, conv_one, bias_one, gain_two, conv_two, bias_two
):
    frame_count = frames_in.shape[0]
    tm_count = lax.axis_size("tm")
    my_block = lax.axis_index("tm")
    target = slot_frame // frame_count
    local_index = slot_frame % frame_count
    member = (target[:, None] == jnp.arange(tm_count)[None, :]).astype(jnp.int32)
    ranked = jnp.sum(member * (jnp.cumsum(member, axis=0) - 1), axis=1)
    bucket_of = target * CAP + ranked
    matched = bucket_of[None, :] == jnp.arange(tm_count * CAP)[:, None]
    chosen = jnp.sum(jnp.where(matched, jnp.arange(frame_count)[None, :], 0), axis=1)
    filled = jnp.any(matched, axis=1)
    packed = jnp.where(
        filled[:, None, None, None],
        jnp.take(frames_in, chosen, axis=0),
        jnp.zeros((), frames_in.dtype),
    )
    labels = jnp.where(filled, jnp.take(local_index, chosen), -1).astype(jnp.bfloat16)
    packed = packed.reshape((tm_count, CAP) + frames_in.shape[1:])
    labels = labels.reshape(tm_count, CAP)
    arrived, arrived_labels = (
        lax.all_to_all(packed, "tm", split_axis=0, concat_axis=0, tiled=True),
        lax.all_to_all(labels, "tm", split_axis=0, concat_axis=0, tiled=True),
    )
    arrived = arrived.reshape((tm_count * CAP,) + frames_in.shape[1:])
    arrived_labels = arrived_labels.reshape(-1).astype(jnp.int32)
    matches = arrived_labels[None, :] == jnp.arange(frame_count)[:, None]
    picked = jnp.sum(jnp.where(matches, jnp.arange(tm_count * CAP)[None, :], 0), axis=1)
    video = jnp.take(arrived, picked, axis=0)
    starts = jnp.cumsum(shot_spans) - shot_spans
    span_ids = my_block * (frame_count // SPAN) + jnp.arange(frame_count // SPAN)
    opened = jnp.any(starts[None, :] == span_ids[:, None], axis=1)
    first = norm_silu(video, gain_one).astype(jnp.bfloat16)
    earlier = shifted_2(first[-2:], "tm", 1)
    extended = row_rims(jnp.concatenate([earlier, first], axis=0))
    hidden = causal_conv(extended, conv_one, bias_one, opened, frame_count)
    second = norm_silu(hidden, gain_two).astype(jnp.bfloat16)
    earlier_two = shifted_2(second[-2:], "tm", 1)
    extended_two = row_rims(jnp.concatenate([earlier_two, second], axis=0))
    branch = causal_conv(extended_two, conv_two, bias_two, opened, frame_count)
    return (video.astype(jnp.float32) + branch).astype(jnp.bfloat16)


def solution(mesh):
    placed = (P("tm", "rows", None, None), P("tm"), P(), P(), P(), P(), P(), P(), P())
    return jax.shard_map(
        body, mesh=mesh, in_specs=placed, out_specs=P("tm", "rows", None, None), check_vma=False
    )
```

profile of v0, /device:TPU:448, one launch (start us, length us, event | category | flops | bytes accessed | tf_op | source)
XLA Modules:
  0.0 141.9 jit_solution(11225564223688541296)
XLA Ops:
  0.0 0.7 and_select_fusion.2
  1.5 0.7 gather_fusion
  2.4 0.7 copy.25
  3.1 9.5 %all-to-all-start = ((bf16[8,1,2]{2,1,0:T(2,128)(2,1)}), bf16[8,1,2]{2,1,0:T(2,128)(2,1)S(1)}, u32[]{:S(2)}, u32[]{:S(2)}) async-start(bf16[8,1,2]{2,1,0:T(2,128)(2,1)} %copy.25), calls=%async_computation | async-start | bytes 8192 | tf_op jit(solution)/shard_map/all_to_all | solution.py:96
  12.8 0.6 gather_fusion.1
  13.4 0.9 select_select_fusion
  14.5 1.1 all-to-all-done
  15.7 10.6 %all-to-all-start.1 = ((bf16[8,2,2,32,192]{4,3,2,1,0:T(8,128)(2,1)}), bf16[8,2,2,32,192]{4,3,2,1,0:T(8,128)(2,1)S(1)}, u32[]{:S(2)}, u32[]{:S(2)}) async-start(bf16[8,2,2,32,192]{4,3,2,1,0:T(8,128)(2,1)} %select_select_fusion), calls=%async_computation.1 | async-start | bytes 1048576 | tf_op jit(solution)/shard_map/all_to_all | solution.py:95
  26.5 0.6 gather_fusion.3
  27.1 1.5 %fusion.30 = (bf16[1,1,3,192,192]{4,3,2,1,0:T(8,128)(2,1)}, bf16[1,1,3,192,192]{4,3,2,1,0:T(8,128)(2,1)}, bf16[1,1,3,192,192]{4,3,2,1,0:T(8,128)(2,1)}, bf16[1,1...) fusion(bf16[3,3,3,192,192]{4,3,2,1,0:T(8,128)(2,1)S(1)} %copy-d, ...), kind=kLoop, calls=%fused_computation.128 | loop fusion | bytes 3981312 | tf_op jit(solution)/shard_map/slice | solution.py:67
  28.9 17.9 %all-to-all-done.1 = bf16[8,2,2,32,192]{4,3,2,1,0:T(8,128)(2,1)S(1)} async-done(((bf16[8,2,2,32,192]{4,3,2,1,0:T(8,128)(2,1)}), bf16[8,2,2,32,192]{4,3,2,1,0:T(8,128)(2,1)S(1)}, u32[]{:S(2)}, u32[]{:S(2)}) %all-to-all-start.1) | async-done | bytes 393248 | tf_op jit(solution)/shard_map/all_to_all | solution.py:95
  46.9 0.6 gather_fusion.2
  48.0 4.7 %collective-permute-start = (bf16[2,2,32,192]{3,2,1,0:T(8,128)(2,1)S(1)}, bf16[2,2,32,192]{3,2,1,0:T(8,128)(2,1)S(1)}, u32[]{:S(2)}, u32[]{:S(2)}) collective-permute-start(bf16[2,2,32,192]{3,2,1,0:T(8,128)(2,1)S(1)} %slice.416), channel_id=1, source_target_pairs={{0,64},{64,128},{128,192},{192,256},{256,320},{320,384},{384,448},... | collective-permute-start | bytes 147464 | tf_op jit(solution)/shard_map/ppermute | solution.py:30
  52.7 1.9 %collective-permute-done = bf16[2,2,32,192]{3,2,1,0:T(8,128)(2,1)S(1)} collective-permute-done((bf16[2,2,32,192]{3,2,1,0:T(8,128)(2,1)S(1)}, bf16[2,2,32,192]{3,2,1,0:T(8,128)(2,1)S(1)}, u32[]{:S(2)}, u32[]{:S(2)}) %collective-permute-start) | collective-permute-done | bytes 49184 | tf_op jit(solution)/shard_map/ppermute | solution.py:30
  54.7 8.8 %collective-permute-start.2 = (bf16[10,1,32,192]{3,2,1,0:T(8,128)(2,1)S(1)}, bf16[10,1,32,192]{3,2,1,0:T(8,128)(2,1)S(1)}, u32[]{:S(2)}, u32[]{:S(2)}) collective-permute-start(bf16[10,1,32,192]{3,2,1,0:T(8,128)(2,1)S(1)} %get-tuple-element.89), channel_id=1, source_target_pairs={{1,0},{2,1},{3,2},{4,3},{5,4},{6,5},{7,6},{8,7},{9,8},{10,9},{11,1... | collective-permute-start | bytes 368648 | tf_op jit(solution)/shard_map/ppermute | solution.py:20
  63.4 1.9 %collective-permute-start.1 = (bf16[10,1,32,192]{3,2,1,0:T(8,128)(2,1)S(1)}, bf16[10,1,32,192]{3,2,1,0:T(8,128)(2,1)S(1)}, u32[]{:S(2)}, u32[]{:S(2)}) collective-permute-start(bf16[10,1,32,192]{3,2,1,0:T(8,128)(2,1)S(1)} %get-tuple-element.88), channel_id=1, source_target_pairs={{0,1},{1,2},{2,3},{3,4},{4,5},{5,6},{6,7},{7,8},{8,9},{9,10},{10,1... | collective-permute-start | bytes 368648 | tf_op jit(solution)/shard_map/ppermute | solution.py:18
  65.4 5.2 %collective-permute-done.2 = bf16[10,1,32,192]{3,2,1,0:T(8,128)(2,1)S(1)} collective-permute-done((bf16[10,1,32,192]{3,2,1,0:T(8,128)(2,1)S(1)}, bf16[10,1,32,192]{3,2,1,0:T(8,128)(2,1)S(1)}, u32[]{:S(2)}, u32[]{:S(2)}) %collective-permute-start.2) | collective-permute-done | bytes 122912 | tf_op jit(solution)/shard_map/ppermute | solution.py:20
  70.6 16.8 %collective-permute-done.1 = bf16[10,1,32,192]{3,2,1,0:T(8,128)(2,1)S(1)} collective-permute-done((bf16[10,1,32,192]{3,2,1,0:T(8,128)(2,1)S(1)}, bf16[10,1,32,192]{3,2,1,0:T(8,128)(2,1)S(1)}, u32[]{:S(2)}, u32[]{:S(2)}) %collective-permute-start.1) | collective-permute-done | bytes 122912 | tf_op jit(solution)/shard_map/ppermute | solution.py:18
  88.5 0.5 pad_maximum_fusion
  89.0 0.5 copy-done.11
  89.8 1.1 fusion.34
  97.7 1.1 multiply_reduce_fusion
  98.8 2.0 %copy.26 = f32[512,192]{1,0:T(8,128)} copy(f32[512,192]{0,1:T(8,128)} %get-tuple-element.95) | data formatting | bytes 786432 | tf_op jit(solution)/shard_map/add | solution.py:68
  100.9 1.3 multiply_convert_fusion
  102.2 1.9 %collective-permute-start.3 = (bf16[2,2,32,192]{3,2,1,0:T(8,128)(2,1)S(1)}, bf16[2,2,32,192]{3,2,1,0:T(8,128)(2,1)S(1)}, u32[]{:S(2)}, u32[]{:S(2)}) collective-permute-start(bf16[2,2,32,192]{3,2,1,0:T(8,128)(2,1)S(1)} %slice.449), channel_id=1, source_target_pairs={{0,64},{64,128},{128,192},{192,256},{256,320},{320,384},{384,448},... | collective-permute-start | bytes 147464 | tf_op jit(solution)/shard_map/ppermute | solution.py:30
  104.2 4.2 %collective-permute-done.3 = bf16[2,2,32,192]{3,2,1,0:T(8,128)(2,1)S(1)} collective-permute-done((bf16[2,2,32,192]{3,2,1,0:T(8,128)(2,1)S(1)}, bf16[2,2,32,192]{3,2,1,0:T(8,128)(2,1)S(1)}, u32[]{:S(2)}, u32[]{:S(2)}) %collective-permute-start.3) | collective-permute-done | bytes 49184 | tf_op jit(solution)/shard_map/ppermute | solution.py:30
  108.5 1.9 %collective-permute-start.5 = (bf16[10,1,32,192]{3,2,1,0:T(8,128)(2,1)S(1)}, bf16[10,1,32,192]{3,2,1,0:T(8,128)(2,1)S(1)}, u32[]{:S(2)}, u32[]{:S(2)}) collective-permute-start(bf16[10,1,32,192]{3,2,1,0:T(8,128)(2,1)S(1)} %get-tuple-element.87), channel_id=1, source_target_pairs={{1,0},{2,1},{3,2},{4,3},{5,4},{6,5},{7,6},{8,7},{9,8},{10,9},{11,1... | collective-permute-start | bytes 368648 | tf_op jit(solution)/shard_map/ppermute | solution.py:20
  110.4 2.6 %collective-permute-start.4 = (bf16[10,1,32,192]{3,2,1,0:T(8,128)(2,1)S(1)}, bf16[10,1,32,192]{3,2,1,0:T(8,128)(2,1)S(1)}, u32[]{:S(2)}, u32[]{:S(2)}) collective-permute-start(bf16[10,1,32,192]{3,2,1,0:T(8,128)(2,1)S(1)} %get-tuple-element.86), channel_id=1, source_target_pairs={{0,1},{1,2},{2,3},{3,4},{4,5},{5,6},{6,7},{7,8},{8,9},{9,10},{10,1... | collective-permute-start | bytes 368648 | tf_op jit(solution)/shard_map/ppermute | solution.py:18
  113.2 3.1 %collective-permute-done.5 = bf16[10,1,32,192]{3,2,1,0:T(8,128)(2,1)S(1)} collective-permute-done((bf16[10,1,32,192]{3,2,1,0:T(8,128)(2,1)S(1)}, bf16[10,1,32,192]{3,2,1,0:T(8,128)(2,1)S(1)}, u32[]{:S(2)}, u32[]{:S(2)}) %collective-permute-start.5) | collective-permute-done | bytes 122912 | tf_op jit(solution)/shard_map/ppermute | solution.py:20
  116.3 16.8 %collective-permute-done.4 = bf16[10,1,32,192]{3,2,1,0:T(8,128)(2,1)S(1)} collective-permute-done((bf16[10,1,32,192]{3,2,1,0:T(8,128)(2,1)S(1)}, bf16[10,1,32,192]{3,2,1,0:T(8,128)(2,1)S(1)}, u32[]{:S(2)}, u32[]{:S(2)}) %collective-permute-start.4) | collective-permute-done | bytes 122912 | tf_op jit(solution)/shard_map/ppermute | solution.py:18
  134.1 0.4 fusion.32
  141.0 0.8 fusion.19
  (116 shorter events, 18.1 us)
Async XLA Ops:
  0.0 12.7 %copy-start = (bf16[8,2,32,192]{3,2,1,0:T(8,128)(2,1)S(1)}, bf16[8,2,32,192]{3,2,1,0:T(8,128)(2,1)}, u32[]{:S(2)}) copy-start(bf16[8,2,32,192]{3,2,1,0:T(8,128)(2,1)} %param.11) | copy-start | bytes 589828
  1.5 12.9 %copy-start.16 = (s32[4]{0:T(128)S(1)}, s32[4]{0:T(128)}, u32[]{:S(2)}) copy-start(s32[4]{0:T(128)} %param.13) | copy-start | bytes 52
  3.1 12.6 %all-to-all-start = ((bf16[8,1,2]{2,1,0:T(2,128)(2,1)}), bf16[8,1,2]{2,1,0:T(2,128)(2,1)S(1)}, u32[]{:S(2)}, u32[]{:S(2)}) async-start(bf16[8,1,2]{2,1,0:T(2,128)(2,1)} %copy.25), calls=%async_computation | async-start | bytes 8192 | tf_op jit(solution)/shard_map/all_to_all | solution.py:96
  12.7 14.4 %copy-start.1 = (bf16[3,3,3,192,192]{4,3,2,1,0:T(8,128)(2,1)S(1)}, bf16[3,3,3,192,192]{4,3,2,1,0:T(8,128)(2,1)}, u32[]{:S(2)}) copy-start(bf16[3,3,3,192,192]{4,3,2,1,0:T(8,128)(2,1)} %param.15) | copy-start | bytes 5971972
  15.7 31.2 %all-to-all-start.1 = ((bf16[8,2,2,32,192]{4,3,2,1,0:T(8,128)(2,1)}), bf16[8,2,2,32,192]{4,3,2,1,0:T(8,128)(2,1)S(1)}, u32[]{:S(2)}, u32[]{:S(2)}) async-start(bf16[8,2,2,32,192]{4,3,2,1,0:T(8,128)(2,1)} %select_select_fusion), calls=%async_computation.1 | async-start | bytes 1048576 | tf_op jit(solution)/shard_map/all_to_all | solution.py:95
  27.1 20.6 %copy-start.13 = (f32[192]{0:T(256)S(1)}, f32[192]{0:T(256)}, u32[]{:S(2)}) copy-start(f32[192]{0:T(256)} %param.14) | copy-start | bytes 2308
  48.0 6.6 %collective-permute-start = (bf16[2,2,32,192]{3,2,1,0:T(8,128)(2,1)S(1)}, bf16[2,2,32,192]{3,2,1,0:T(8,128)(2,1)S(1)}, u32[]{:S(2)}, u32[]{:S(2)}) collective-permute-start(bf16[2,2,32,192]{3,2,1,0:T(8,128)(2,1)S(1)} %slice.416), channel_id=1, source_target_pairs={{0,64},{64,128},{128,192},{192,256},{256,320},{320,384},{384,448},... | collective-permute-start | bytes 147464 | tf_op jit(solution)/shard_map/ppermute | solution.py:30
  54.7 15.9 %collective-permute-start.2 = (bf16[10,1,32,192]{3,2,1,0:T(8,128)(2,1)S(1)}, bf16[10,1,32,192]{3,2,1,0:T(8,128)(2,1)S(1)}, u32[]{:S(2)}, u32[]{:S(2)}) collective-permute-start(bf16[10,1,32,192]{3,2,1,0:T(8,128)(2,1)S(1)} %get-tuple-element.89), channel_id=1, source_target_pairs={{1,0},{2,1},{3,2},{4,3},{5,4},{6,5},{7,6},{8,7},{9,8},{10,9},{11,1... | collective-permute-start | bytes 368648 | tf_op jit(solution)/shard_map/ppermute | solution.py:20
  63.4 24.0 %collective-permute-start.1 = (bf16[10,1,32,192]{3,2,1,0:T(8,128)(2,1)S(1)}, bf16[10,1,32,192]{3,2,1,0:T(8,128)(2,1)S(1)}, u32[]{:S(2)}, u32[]{:S(2)}) collective-permute-start(bf16[10,1,32,192]{3,2,1,0:T(8,128)(2,1)S(1)} %get-tuple-element.88), channel_id=1, source_target_pairs={{0,1},{1,2},{2,3},{3,4},{4,5},{5,6},{6,7},{7,8},{8,9},{9,10},{10,1... | collective-permute-start | bytes 368648 | tf_op jit(solution)/shard_map/ppermute | solution.py:18
  88.5 1.0 copy-start.11
  89.8 1.1 copy-start.10
  91.0 1.0 copy-start.9
  91.9 1.0 copy-start.8
  92.9 1.0 copy-start.7
  93.8 1.0 copy-start.6
  94.8 1.0 copy-start.5
  95.8 1.0 copy-start.4
  96.7 1.0 copy-start.3
  96.7 1.0 copy-start.12
  97.7 3.2 %copy-start.14 = (f32[192]{0:T(256)S(1)}, f32[192]{0:T(256)}, u32[]{:S(2)}) copy-start(f32[192]{0:T(256)} %param.17) | copy-start | bytes 2308
  97.7 15.3 %copy-start.2 = (bf16[3,3,3,192,192]{4,3,2,1,0:T(8,128)(2,1)S(1)}, bf16[3,3,3,192,192]{4,3,2,1,0:T(8,128)(2,1)}, u32[]{:S(2)}) copy-start(bf16[3,3,3,192,192]{4,3,2,1,0:T(8,128)(2,1)} %param.18) | copy-start | bytes 5971972
  102.2 6.2 %collective-permute-start.3 = (bf16[2,2,32,192]{3,2,1,0:T(8,128)(2,1)S(1)}, bf16[2,2,32,192]{3,2,1,0:T(8,128)(2,1)S(1)}, u32[]{:S(2)}, u32[]{:S(2)}) collective-permute-start(bf16[2,2,32,192]{3,2,1,0:T(8,128)(2,1)S(1)} %slice.449), channel_id=1, source_target_pairs={{0,64},{64,128},{128,192},{192,256},{256,320},{320,384},{384,448},... | collective-permute-start | bytes 147464 | tf_op jit(solution)/shard_map/ppermute | solution.py:30
  108.5 7.8 %collective-permute-start.5 = (bf16[10,1,32,192]{3,2,1,0:T(8,128)(2,1)S(1)}, bf16[10,1,32,192]{3,2,1,0:T(8,128)(2,1)S(1)}, u32[]{:S(2)}, u32[]{:S(2)}) collective-permute-start(bf16[10,1,32,192]{3,2,1,0:T(8,128)(2,1)S(1)} %get-tuple-element.87), channel_id=1, source_target_pairs={{1,0},{2,1},{3,2},{4,3},{5,4},{6,5},{7,6},{8,7},{9,8},{10,9},{11,1... | collective-permute-start | bytes 368648 | tf_op jit(solution)/shard_map/ppermute | solution.py:20
  110.4 22.7 %collective-permute-start.4 = (bf16[10,1,32,192]{3,2,1,0:T(8,128)(2,1)S(1)}, bf16[10,1,32,192]{3,2,1,0:T(8,128)(2,1)S(1)}, u32[]{:S(2)}, u32[]{:S(2)}) collective-permute-start(bf16[10,1,32,192]{3,2,1,0:T(8,128)(2,1)S(1)} %get-tuple-element.86), channel_id=1, source_target_pairs={{0,1},{1,2},{2,3},{3,4},{4,5},{5,6},{6,7},{7,8},{8,9},{9,10},{10,1... | collective-permute-start | bytes 368648 | tf_op jit(solution)/shard_map/ppermute | solution.py:18
  140.3 0.7 copy-start.15
where the time goes:
time: 143 us; the launch traced here: 142 us
  waiting for transfers between devices  67.1 us (47%)
  starting transfers between devices  41.9 us (29%)
  local copies, waits for them, and re-layouts  13.7 us (10%)
  other arithmetic  10.7 us (7%)
  matrix products  7.8 us (5%)
    ppermute x2, waiting for transfers between devices, extended_2(): lax.ppermute(tail, axis, [(i, (i + 1) % count) for i in range(ends)])  33.6 us
    all_to_all x1, waiting for transfers between devices, body(): lax.all_to_all(packed, 'tm', split_axis=0, concat_axis=0, tiled=True)  17.9 us
    ppermute x2, starting transfers between devices, extended_2(): lax.ppermute(head, axis, [((i + 1) % count, i) for i in range(ends)])  10.7 us
    all_to_all x1, starting transfers between devices, body(): lax.all_to_all(packed, 'tm', split_axis=0, concat_axis=0, tiled=True)  10.6 us
    all_to_all x1, starting transfers between devices, body(): lax.all_to_all(labels, 'tm', split_axis=0, concat_axis=0, tiled=True)  9.46 us
    ppermute x2, waiting for transfers between devices, extended_2(): lax.ppermute(head, axis, [((i + 1) % count, i) for i in range(ends)])  8.3 us
    dot_general x18, matrix products, causal_conv(): jnp.dot(stacked, kernel, preferred_element_type=jnp.float32)  7.8 us
    ppermute x2, starting transfers between devices, shifted_2(): return lax.ppermute(block, axis, route)  6.65 us
  transfers between devices with their start and end apart: 8, of which 8 were waited for; matrix products, arithmetic and copies ran while one was open for 3% of the time, Pallas kernels for 0%

commit v1 on v0

v1 whole, which is shorter than its diff:
```python
import functools

import jax
import jax.numpy as jnp
from jax import lax
from jax.experimental import pallas as pl
from jax.experimental.pallas import tpu as pltpu
from jax.sharding import PartitionSpec as P

SPAN = 4
CH = 192
COLS = 32
N_TM = 8
F = 8
PACK = 48
ORDER = (4, 3, 5, 2, 6, 1, 7)
F32 = jnp.float32
BF16 = jnp.bfloat16
MESH = pl.DeviceIdType.MESH


def remote(src, dst, send, recv, tm, rows):
    return pltpu.make_async_remote_copy(
        src_ref=src, dst_ref=dst, send_sem=send, recv_sem=recv, device_id=(tm, rows), device_id_type=MESH
    )


def silu(u):
    return u / (1.0 + jnp.exp(-u))


def spread(packed):
    low, pairs = packed[:COLS], packed[COLS:]
    high = jnp.concatenate([pairs[:, :64], pairs[:, 64:]], axis=0)
    return jnp.concatenate([low, high], axis=1)


def gathered(image_row):
    high = image_row[:, 128:]
    pairs = jnp.concatenate([high[:16], high[16:]], axis=1)
    return jnp.concatenate([image_row[:, :128], pairs], axis=0)


def norm_packed(packed, gain_low, gain_pairs):
    low, pairs = packed[:COLS], packed[COLS:]
    left = lax.broadcasted_iota(jnp.int32, pairs.shape, 1) < 64
    low_sum = jnp.sum(low * low, axis=-1, keepdims=True)
    squares = pairs * pairs
    left_sum = jnp.sum(jnp.where(left, squares, 0.0), axis=-1, keepdims=True)
    both_sum = jnp.sum(squares, axis=-1, keepdims=True)
    total = low_sum + jnp.concatenate([left_sum, both_sum - left_sum], axis=0)
    scale = lax.rsqrt(total * (1.0 / CH) + 1e-06)
    low_out = silu(low * scale * gain_low)
    pairs_out = silu(pairs * jnp.where(left, scale[:16], scale[16:]) * gain_pairs)
    return low_out, pairs_out


def col_taps(left, middle, right):
    count = middle.shape[0]
    col = lax.broadcasted_iota(jnp.int32, middle.shape, 0) % COLS
    from_left = jnp.where(col == 0, 0.0, pltpu.roll(left, 1, 0))
    from_right = jnp.where(col == COLS - 1, 0.0, pltpu.roll(right, count - 1, 0))
    return middle + from_left + from_right


def conv(source, base, frames, rows, weight):
    count = frames * rows * COLS
    sums = [jnp.zeros((count, CH), F32) for _ in range(3)]
    for time_tap in range(3):
        for row_tap in range(3):
            tile = source[pl.ds(base + time_tap, frames), pl.ds(row_tap, rows)].reshape(count, CH)
            for col_tap in range(3):
                tap = weight[(time_tap * 3 + row_tap) * 3 + col_tap]
                sums[col_tap] = sums[col_tap] + jnp.dot(tile, tap, preferred_element_type=F32)
    return col_taps(*sums)


def kernel(
    n_rows,
    frames, slots, slots_v, spans, gain_low, gain_pairs, gain_two, bias_one, bias_two, conv_one, conv_two,
    out,
    w_one, w_two, packed, outgoing, arrived, labels, labels_s, video, own, up, down, before, before_up, before_down,
    grid_one, grid_two,
    w_sem, label_sem, a_send, a_recv, l_send, l_recv, h_send, h_recv,
):
    me = lax.axis_index("tm")
    row = lax.axis_index("rows")
    has_up, has_down = row > 0, row < n_rows - 1
    has_next, has_before = me < N_TM - 1, me > 0

    load_one = pltpu.make_async_copy(conv_one, w_one, w_sem.at[0])
    load_two = pltpu.make_async_copy(conv_two, w_two, w_sem.at[1])
    load_one.start()
    load_two.start()

    barrier = pltpu.get_barrier_semaphore()
    for step in range(1, N_TM):
        pl.semaphore_signal(barrier, inc=1, device_id=(lax.rem(me + step, N_TM), row), device_id_type=MESH)
    peers = jnp.int32(N_TM - 1)
    for has_row, row_step in ((has_up, -1), (has_down, 1)):
        for has_tm, tm_step in ((None, 0), (has_next, 1), (has_before, -1)):
            there = has_row if has_tm is None else jnp.logical_and(has_row, has_tm)
            peers = peers + there.astype(jnp.int32)

            @pl.when(there)
            def _():
                pl.semaphore_signal(
                    barrier, inc=1, device_id=(me + tm_step, row + row_step), device_id_type=MESH
                )

    for slot in range(F):
        for line in range(2):
            packed[slot, line * PACK : (line + 1) * PACK] = gathered(frames[slot, line])
    for step in range(N_TM):
        target = lax.rem(me + step, N_TM)
        count = jnp.int32(0)
        picks = [jnp.int32(0), jnp.int32(0)]
        for slot in range(F):
            mine = lax.shift_right_logical(slots[slot], 3) == target
            for rank in range(2):
                picks[rank] = jnp.where(jnp.logical_and(mine, count == rank), slot, picks[rank])
            count = count + mine.astype(jnp.int32)
        for rank in range(2):
            block = packed[picks[rank]]
            if step:
                outgoing[2 * step + rank] = block
            else:
                arrived[rank] = block

    pl.semaphore_wait(barrier, peers)

    label_copies, frame_copies = {}, {}
    for step in ORDER:
        label_copies[step] = remote(
            slots_v.at[pl.ds(0, 1)], labels.at[pl.ds(step, 1)], l_send.at[step], l_recv.at[step],
            lax.rem(me + step, N_TM), row,
        )
        label_copies[step].start()
    for step in ORDER:
        frame_copies[step] = remote(
            outgoing.at[pl.ds(2 * step, 2)], arrived.at[pl.ds(2 * step, 2)], a_send.at[step], a_recv.at[step],
            lax.rem(me + step, N_TM), row,
        )
        frame_copies[step].start()

    @pl.when(jnp.logical_not(has_up))
    def _():
        up[...] = jnp.zeros_like(up)
        before_up[...] = jnp.zeros_like(before_up)

    @pl.when(jnp.logical_not(has_down))
    def _():
        down[...] = jnp.zeros_like(down)
        before_down[...] = jnp.zeros_like(before_down)

    @pl.when(jnp.logical_not(has_before))
    def _():
        before[...] = jnp.zeros_like(before)
        before_up[...] = jnp.zeros_like(before_up)
        before_down[...] = jnp.zeros_like(before_down)

    labels[0:1] = slots_v[0:1]
    for step in ORDER:
        label_copies[step].wait()
    to_scalars = pltpu.make_async_copy(labels, labels_s, label_sem)
    to_scalars.start()
    to_scalars.wait()

    def scan_source(step, places):
        count = jnp.int32(0)
        for slot in range(F):
            held = labels_s[step, slot]
            mine = lax.shift_right_logical(held, 3) == me
            local = jnp.bitwise_and(held, F - 1)
            places = tuple(
                jnp.where(jnp.logical_and(mine, local == f), 2 * step + jnp.minimum(count, 1), places[f]) for f in range(F)
            )
            count = count + mine.astype(jnp.int32)
        return places

    places = lax.fori_loop(0, N_TM, scan_source, (jnp.int32(0),) * F)

    opened = []
    for span in range(2):
        start, hit = jnp.int32(0), jnp.bool_(False)
        for shot in range(4):
            hit = jnp.logical_or(hit, start == 2 * me + span)
            start = start + spans[shot]
        opened.append(hit)
    keep = [jnp.where(hit, 0.0, 1.0).astype(BF16) for hit in opened]

    for step in ORDER:
        frame_copies[step].wait()

    for f in range(F):
        block = arrived[places[f]]
        for line in range(2):
            part = block[line * PACK : (line + 1) * PACK]
            video[f, line] = spread(part)
            low, pairs = norm_packed(part.astype(F32), gain_low[...], gain_pairs[...])
            own[f, line * PACK : line * PACK + COLS] = low.astype(BF16)
            own[f, line * PACK + COLS : (line + 1) * PACK] = pairs.astype(BF16)

    last = pl.ds(F - SPAN, SPAN)
    sends = (
        (has_up, own, down, 0, 0, -1),
        (has_down, own, up, 1, 0, 1),
        (jnp.logical_and(has_next, has_up), own.at[last], before_down, 2, 1, -1),
        (jnp.logical_and(has_next, has_down), own.at[last], before_up, 3, 1, 1),
        (has_next, own.at[last], before, 4, 1, 0),
    )
    arrivals = (has_down, has_up, jnp.logical_and(has_before, has_down), jnp.logical_and(has_before, has_up), has_before)
    halos = [
        remote(src, dst, h_send.at[i], h_recv.at[i], me + tm_step, row + row_step)
        for _, src, dst, i, tm_step, row_step in sends
    ]
    for (there, *_), copy in zip(sends, halos):

        @pl.when(there)
        def _():
            copy.start()

    def place(f, lines, base, source, keep_one):
        for line in range(2):
            value = spread(source[lines, line * PACK : (line + 1) * PACK])
            grid_one[(8 if f >= SPAN else 6) + f, base + line] = value
            if f in (2, 3):
                grid_one[8 + f, base + line] = jnp.where(opened[1], jnp.zeros_like(value), value)

    def place_before(f, base, source):
        for line in range(2):
            value = spread(source[f, line * PACK : (line + 1) * PACK])
            grid_one[f, base + line] = value
            if f in (2, 3):
                grid_one[2 + f, base + line] = jnp.where(opened[0], jnp.zeros_like(value), value)

    for f in range(F):
        place(f, f, 2, own, keep)

    for there, copy in zip(arrivals, halos):

        @pl.when(there)
        def _():
            copy.wait_recv()

    for f in range(F):
        place(f, f, 0, up, keep)
        place(f, f, 4, down, keep)
    for f in range(SPAN):
        place_before(f, 2, before)
        place_before(f, 0, before_up)
        place_before(f, 4, before_down)

    load_one.wait()

    line_of = lax.broadcasted_iota(jnp.int32, (2 * 4 * COLS, 1), 0) // COLS % 4
    outside = jnp.logical_or(
        jnp.logical_and(line_of == 0, jnp.logical_not(has_up)),
        jnp.logical_and(line_of == 3, jnp.logical_not(has_down)),
    )
    for pair, base in enumerate((0, 4, 6, 10, 12)):
        hidden = conv(grid_one, base, 2, 4, w_one) + bias_one[...]
        mean = jnp.sum(hidden * hidden, axis=-1, keepdims=True) * (1.0 / CH)
        second = silu(hidden * lax.rsqrt(mean + 1e-06) * gain_two[...])
        second = jnp.where(outside, 0.0, second).astype(BF16).reshape(2, 4, COLS, CH)
        if pair == 0:
            grid_two[0:2] = jnp.where(opened[0], jnp.zeros_like(second), second)
        else:
            at = 2 * pair if pair < 3 else 2 * pair + 2
            grid_two[at : at + 2] = second
            if pair == 2:
                grid_two[6:8] = jnp.where(opened[1], jnp.zeros_like(second), second)

    load_two.wait()
    for span in range(2):
        branch = conv(grid_two, 6 * span, SPAN, 2, w_two) + bias_two[...]
        held = video[SPAN * span : SPAN * (span + 1)].astype(F32)
        out[SPAN * span : SPAN * (span + 1)] = (held + branch.reshape(SPAN, 2, COLS, CH)).astype(BF16)

    for (there, *_), copy in zip(sends, halos):

        @pl.when(there)
        def _():
            copy.wait_send()


def body(
    frames_in, slot_frame, shot_spans, gain_one, conv_one, bias_one, gain_two, conv_two, bias_two
):
    slots_v = jnp.broadcast_to(jnp.pad(slot_frame, (0, 128 - F))[None, :], (8, 128))
    gain_low = gain_one[None, :128]
    gain_pairs = jnp.concatenate([gain_one[128:], gain_one[128:]])[None, :]
    vmem = pl.BlockSpec(memory_space=pltpu.VMEM)
    smem = pl.BlockSpec(memory_space=pltpu.SMEM)
    hbm = pl.BlockSpec(memory_space=pl.ANY)
    dma = pltpu.SemaphoreType.DMA
    taps = (27, CH, CH)
    whole, tail = (F, 2 * PACK, 128), (SPAN, 2 * PACK, 128)
    return pl.pallas_call(
        functools.partial(kernel, lax.axis_size("rows")),
        out_shape=jax.ShapeDtypeStruct(frames_in.shape, BF16),
        in_specs=[vmem, smem, vmem, smem, vmem, vmem, vmem, vmem, vmem, hbm, hbm],
        out_specs=vmem,
        scratch_shapes=[
            pltpu.VMEM(taps, BF16),
            pltpu.VMEM(taps, BF16),
            pltpu.VMEM(whole, BF16),
            pltpu.VMEM((2 * N_TM, 2 * PACK, 128), BF16),
            pltpu.VMEM((2 * N_TM, 2 * PACK, 128), BF16),
            pltpu.VMEM((8, 128), jnp.int32),
            pltpu.SMEM((8, 128), jnp.int32),
            pltpu.VMEM((F, 2, COLS, CH), BF16),
            pltpu.VMEM(whole, BF16),
            pltpu.VMEM(whole, BF16),
            pltpu.VMEM(whole, BF16),
            pltpu.VMEM(tail, BF16),
            pltpu.VMEM(tail, BF16),
            pltpu.VMEM(tail, BF16),
            pltpu.VMEM((16, 6, COLS, CH), BF16),
            pltpu.VMEM((12, 4, COLS, CH), BF16),
            dma((2,)),
            dma,
            dma((N_TM,)),
            dma((N_TM,)),
            dma((N_TM,)),
            dma((N_TM,)),
            dma((5,)),
            dma((5,)),
        ],
        name="residual_block",
        compiler_params=pltpu.CompilerParams(
            collective_id=1, has_side_effects=True, vmem_limit_bytes=40 << 20
        ),
    )(
        frames_in, slot_frame, slots_v, shot_spans, gain_low, gain_pairs, gain_two[None, :],
        bias_one[None, :], bias_two[None, :], conv_one.reshape(taps), conv_two.reshape(taps),
    )


def solution(mesh):
    placed = (P("tm", "rows", None, None), P("tm"), P(), P(), P(), P(), P(), P(), P())
    return jax.shard_map(
        body, mesh=mesh, in_specs=placed, out_specs=P("tm", "rows", None, None), check_vma=False
    )
```

time: 143 us -> 71.4 us (0.50)
  the two profiles are of different devices: /device:TPU:448 before, /device:TPU:63 now
where the time goes in v1:
time: 71.4 us; the launch traced here: 71 us
  Pallas kernels  60.4 us (85%)
  local copies, waits for them, and re-layouts  9.84 us (14%)
  other arithmetic  0.75 us (1%)
    pallas_call x1, Pallas kernels, body(): pl.pallas_call(functools.partial(kernel, lax.axis_size('rows')), out_shap...  60.4 us
    unnamed x17, local copies, waits for them, and re-layouts  8.5 us

profile of v1, /device:TPU:63, one launch (start us, length us, event | category | flops | bytes accessed | tf_op | source)
XLA Modules:
  0.0 71.0 jit_solution(16781577773622383471)
XLA Ops:
  0.0 0.7 pad.4
  0.7 0.7 slice.8
  1.3 0.8 %maximum_bitcast_fusion = (f32[1,128]{1,0:T(1,128)S(1)}, f32[1,128]{1,0:T(1,128)S(1)}) fusion(f32[64]{0:T(128)S(1)} %slice.8, f32[192]{0:T(256)} %param.12), kind=kLoop, calls=%fused_computation | loop fusion | flops 128 | bytes 1792 | tf_op jit(solution)/shard_map/broadcast_in_dim | solution.py:292
  2.1 0.0 copy-start
  2.1 1.7 %copy-done = bf16[3,3,3,192,192]{4,3,2,1,0:T(8,128)(2,1)S(1)} copy-done((bf16[3,3,3,192,192]{4,3,2,1,0:T(8,128)(2,1)S(1)}, bf16[3,3,3,192,192]{4,3,2,1,0:T(8,128)(2,1)}, u32[]{:S(2)}) %copy-start) | copy-done | bytes 1990680
  3.8 0.0 copy-start.1
  3.8 1.7 %copy-done.1 = bf16[3,3,3,192,192]{4,3,2,1,0:T(8,128)(2,1)S(1)} copy-done((bf16[3,3,3,192,192]{4,3,2,1,0:T(8,128)(2,1)S(1)}, bf16[3,3,3,192,192]{4,3,2,1,0:T(8,128)(2,1)}, u32[]{:S(2)}) %copy-start.1) | copy-done | bytes 1990680
  5.6 0.0 copy-start.2
  5.6 0.9 %copy-done.2 = bf16[8,2,32,192]{3,2,1,0:T(8,128)(2,1)S(1)} copy-done((bf16[8,2,32,192]{3,2,1,0:T(8,128)(2,1)S(1)}, bf16[8,2,32,192]{3,2,1,0:T(8,128)(2,1)}, u32[]{:S(2)}) %copy-start.2) | copy-done | bytes 196632
  6.5 0.0 copy-start.3
  6.5 0.7 copy-done.3
  7.2 0.0 copy-start.4
  7.2 0.7 copy-done.4
  7.9 0.0 copy-start.5
  7.9 0.7 copy-done.5
  8.6 0.0 copy-start.6
  8.6 0.7 copy-done.6
  9.2 0.0 copy-start.7
  9.2 0.7 copy-done.7
  9.9 60.4 %residual_block.1 = bf16[8,2,32,192]{3,2,1,0:T(8,128)(2,1)S(1)} custom-call(bf16[8,2,32,192]{3,2,1,0:T(8,128)(2,1)S(1)} %copy-done.2, s32[8]{0:T(128)S(1)} %copy-done.6, s32[8,128]{1,0:T(8,128)S(1)} %broadcast_in_dim.21.slots_v, s32[4]{0:T(128)S(1)} %copy-done.7, f32[1,128]{1,0:T(1,128)S(1)} %get-tuple-element.6.gain_low, ...), custom_call_target="tpu_custom_call" | custom-call | tf_op jit(solution)/shard_map/residual_block/pallas_call | solution.py:299
  70.3 0.7 copy.11
  (1 shorter events, 0.0 us)
Async XLA Ops:
  2.1 1.7 %copy-start = (bf16[3,3,3,192,192]{4,3,2,1,0:T(8,128)(2,1)S(1)}, bf16[3,3,3,192,192]{4,3,2,1,0:T(8,128)(2,1)}, u32[]{:S(2)}) copy-start(bf16[3,3,3,192,192]{4,3,2,1,0:T(8,128)(2,1)} %param.13) | copy-start | bytes 5971972
  3.8 1.7 %copy-start.1 = (bf16[3,3,3,192,192]{4,3,2,1,0:T(8,128)(2,1)S(1)}, bf16[3,3,3,192,192]{4,3,2,1,0:T(8,128)(2,1)}, u32[]{:S(2)}) copy-start(bf16[3,3,3,192,192]{4,3,2,1,0:T(8,128)(2,1)} %param.16) | copy-start | bytes 5971972
  5.6 0.9 %copy-start.2 = (bf16[8,2,32,192]{3,2,1,0:T(8,128)(2,1)S(1)}, bf16[8,2,32,192]{3,2,1,0:T(8,128)(2,1)}, u32[]{:S(2)}) copy-start(bf16[8,2,32,192]{3,2,1,0:T(8,128)(2,1)} %frames.1) | copy-start | bytes 589828
  6.5 0.7 copy-start.3
  7.2 0.7 copy-start.4
  7.9 0.7 copy-start.5
  8.6 0.7 copy-start.6
  9.2 0.7 copy-start.7

commit v2 on v1

v2 whole, which is shorter than its diff:
```python
import functools

import jax
import jax.numpy as jnp
from jax import lax
from jax.experimental import pallas as pl
from jax.experimental.pallas import tpu as pltpu
from jax.sharding import PartitionSpec as P

SPAN = 4
CH = 192
COLS = 32
N_TM = 8
F = 8
PACK = 48
ORDER = (4, 3, 5, 2, 6, 1, 7)
F32 = jnp.float32
BF16 = jnp.bfloat16
MESH = pl.DeviceIdType.MESH


def remote(src, dst, send, recv, tm, rows):
    return pltpu.make_async_remote_copy(
        src_ref=src, dst_ref=dst, send_sem=send, recv_sem=recv, device_id=(tm, rows), device_id_type=MESH
    )


def silu(u):
    return u / (1.0 + jnp.exp(-u))


def spread(packed):
    low, pairs = packed[:COLS], packed[COLS:]
    high = jnp.concatenate([pairs[:, :64], pairs[:, 64:]], axis=0)
    return jnp.concatenate([low, high], axis=1)


def gathered(image_row):
    high = image_row[:, 128:]
    pairs = jnp.concatenate([high[:16], high[16:]], axis=1)
    return jnp.concatenate([image_row[:, :128], pairs], axis=0)


def norm_packed(packed, gain_low, gain_pairs):
    values = packed.astype(F32)
    low, pairs = values[:COLS], values[COLS:]
    left = lax.broadcasted_iota(jnp.int32, pairs.shape, 1) < 64
    low_sum = jnp.sum(low * low, axis=-1, keepdims=True)
    squares = pairs * pairs
    left_sum = jnp.sum(jnp.where(left, squares, 0.0), axis=-1, keepdims=True)
    right_sum = jnp.sum(jnp.where(left, 0.0, squares), axis=-1, keepdims=True)
    total = low_sum + jnp.concatenate([left_sum, right_sum], axis=0)
    scale = lax.rsqrt(total * (1.0 / CH) + 1e-06)
    low_out = silu(low * scale * gain_low)
    pairs_out = silu(pairs * jnp.where(left, scale[:16], scale[16:]) * gain_pairs)
    return jnp.concatenate([low_out.astype(BF16), pairs_out.astype(BF16)], axis=0)


def col_taps(left, middle, right):
    count = middle.shape[0]
    col = lax.broadcasted_iota(jnp.int32, middle.shape, 0) % COLS
    from_left = jnp.where(col == 0, 0.0, pltpu.roll(left, 1, 0))
    from_right = jnp.where(col == COLS - 1, 0.0, pltpu.roll(right, count - 1, 0))
    return middle + from_left + from_right


def conv(source, base, frames, rows, weight):
    count = frames * rows * COLS
    sums = [jnp.zeros((count, CH), F32) for _ in range(3)]
    for time_tap in range(3):
        for row_tap in range(3):
            tile = source[pl.ds(base + time_tap, frames), pl.ds(row_tap, rows)].reshape(count, CH)
            for col_tap in range(3):
                tap = weight[(time_tap * 3 + row_tap) * 3 + col_tap]
                sums[col_tap] = sums[col_tap] + jnp.dot(tile, tap, preferred_element_type=F32)
    return col_taps(*sums)


def kernel(
    n_rows,
    frames_h, slots, spans, gain_one, conv_one_h, bias_one, gain_two, conv_two_h, bias_two,
    out,
    frames, w_one, w_two,
    packed, packed_first, outgoing, outgoing_first, arrived, first, up_first, down_first,
    labels, labels_s, tail, tail_before, second_tail, second_before, grid_one, grid_two,
    in_sem, label_sem, l_send, l_recv, a_send, a_recv, up_send, up_recv, down_send, down_recv,
    t_send, t_recv, s_send, s_recv,
):
    me = lax.axis_index("tm")
    row = lax.axis_index("rows")
    has_up, has_down = row > 0, row < n_rows - 1
    has_next, has_before = me < N_TM - 1, me > 0
    far_up, far_down = row == n_rows, row == n_rows
    near_up = jnp.logical_and(has_up, jnp.logical_not(far_up))
    near_down = jnp.logical_and(has_down, jnp.logical_not(far_down))

    loads = [
        pltpu.make_async_copy(src, dst, in_sem.at[i])
        for i, (src, dst) in enumerate((
            (frames_h, frames), (conv_one_h, w_one), (conv_two_h, w_two),
        ))
    ]
    for load in loads:
        load.start()

    barrier = pltpu.get_barrier_semaphore()
    for step in range(1, N_TM):
        pl.semaphore_signal(barrier, inc=1, device_id=(lax.rem(me + step, N_TM), row), device_id_type=MESH)
    peers = jnp.int32(N_TM - 1)
    for near, far, row_step in ((near_up, far_up, -1), (near_down, far_down, 1)):
        peers = peers + near.astype(jnp.int32) + N_TM * far.astype(jnp.int32)

        @pl.when(near)
        def _():
            pl.semaphore_signal(barrier, inc=1, device_id=(me, row + row_step), device_id_type=MESH)

        @pl.when(far)
        def _():
            for tm in range(N_TM):
                pl.semaphore_signal(barrier, inc=1, device_id=(tm, row + row_step), device_id_type=MESH)

    lane = lax.broadcasted_iota(jnp.int32, (1, 128), 1)
    held = jnp.zeros((1, 128), jnp.int32)
    for slot in range(F):
        held = jnp.where(lane == slot, slots[slot], held)
    labels[0:1] = held

    loads[0].wait()
    gain = gain_one[...]
    gain_low = gain[:, :128]
    gain_pairs = jnp.concatenate([gain[:, 128:], gain[:, 128:]], axis=1)
    for slot in range(F):
        for line in range(2):
            span_of = slice(line * PACK, (line + 1) * PACK)
            block = gathered(frames[slot, line])
            packed[slot, span_of] = block
            packed_first[slot, span_of] = norm_packed(block, gain_low, gain_pairs)
    for step in range(N_TM):
        target = lax.rem(me + step, N_TM)
        count = jnp.int32(0)
        picks = [jnp.int32(0), jnp.int32(0)]
        for slot in range(F):
            mine = lax.shift_right_logical(slots[slot], 3) == target
            for rank in range(2):
                picks[rank] = jnp.where(jnp.logical_and(mine, count == rank), slot, picks[rank])
            count = count + mine.astype(jnp.int32)
        for rank in range(2):
            at = 2 * step + rank
            outgoing_first[at] = packed_first[picks[rank]]
            if step:
                outgoing[at] = packed[picks[rank]]
            else:
                arrived[rank] = packed[picks[rank]]
                first[rank] = packed_first[picks[rank]]

    pl.semaphore_wait(barrier, peers)

    def pair_of(ref, step):
        return ref.at[pl.ds(2 * step, 2)]

    label_copies, frame_copies, up_near, up_far, down_near, down_far = {}, {}, {}, {}, {}, {}
    for step in range(N_TM):
        target = lax.rem(me + step, N_TM)
        if step:
            label_copies[step] = remote(
                labels.at[pl.ds(0, 1)], labels.at[pl.ds(step, 1)], l_send.at[step], l_recv.at[step], target, row
            )
            frame_copies[step] = remote(
                pair_of(outgoing, step), pair_of(arrived, step), a_send.at[step], a_recv.at[step], target, row
            )
        up_near[step] = remote(
            pair_of(first, step), pair_of(down_first, step), up_send.at[step], up_recv.at[step], me, row - 1
        )
        down_near[step] = remote(
            pair_of(first, step), pair_of(up_first, step), down_send.at[step], down_recv.at[step], me, row + 1
        )
        up_far[step] = remote(
            pair_of(outgoing_first, step), pair_of(down_first, step), up_send.at[step], up_recv.at[step],
            target, row - 1,
        )
        down_far[step] = remote(
            pair_of(outgoing_first, step), pair_of(up_first, step), down_send.at[step], down_recv.at[step],
            target, row + 1,
        )

    def forward(step):
        @pl.when(near_up)
        def _():
            up_near[step].start()

        @pl.when(near_down)
        def _():
            down_near[step].start()

    for step in ORDER:
        label_copies[step].start()
    for step in ORDER:
        frame_copies[step].start()
    for far, copies in ((far_up, up_far), (far_down, down_far)):

        @pl.when(far)
        def _():
            for step in ORDER + (0,):
                copies[step].start()

    forward(0)

    @pl.when(jnp.logical_not(has_up))
    def _():
        up_first[...] = jnp.zeros_like(up_first)

    @pl.when(jnp.logical_not(has_down))
    def _():
        down_first[...] = jnp.zeros_like(down_first)

    @pl.when(jnp.logical_not(has_before))
    def _():
        tail_before[...] = jnp.zeros_like(tail_before)
        second_before[...] = jnp.zeros_like(second_before)

    for step in ORDER:
        label_copies[step].wait_recv()
    to_scalars = pltpu.make_async_copy(labels, labels_s, label_sem)
    to_scalars.start()
    to_scalars.wait()

    def scan_source(step, places):
        count = jnp.int32(0)
        for slot in range(F):
            held = labels_s[step, slot]
            mine = lax.shift_right_logical(held, 3) == me
            local = jnp.bitwise_and(held, F - 1)
            at = 2 * step + jnp.minimum(count, 1)
            places = tuple(jnp.where(jnp.logical_and(mine, local == f), at, places[f]) for f in range(F))
            count = count + mine.astype(jnp.int32)
        return places

    places = lax.fori_loop(0, N_TM, scan_source, (jnp.int32(0),) * F)

    opened = []
    for span in range(2):
        start, hit = jnp.int32(0), jnp.bool_(False)
        for shot in range(4):
            hit = jnp.logical_or(hit, start == 2 * me + span)
            start = start + spans[shot]
        opened.append(hit)

    for step in ORDER:
        frame_copies[step].wait_recv()
        for rank in range(2):
            for line in range(2):
                span_of = slice(line * PACK, (line + 1) * PACK)
                first[2 * step + rank, span_of] = norm_packed(
                    arrived[2 * step + rank, span_of], gain_low, gain_pairs
                )
        forward(step)

    def tail_copy(side):
        return remote(tail.at[side], tail_before.at[side], t_send.at[side], t_recv.at[side], me + 1, row)

    for k in range(2):
        tail[0, k] = first[places[F - 2 + k]]

    @pl.when(has_next)
    def _():
        tail_copy(0).start()

    for has_side, copies in ((has_down, up_near), (has_up, down_near)):

        @pl.when(has_side)
        def _():
            for step in (0,) + ORDER:
                copies[step].wait_recv()

    for k in range(2):
        tail[1, k] = up_first[places[F - 2 + k]]
        tail[2, k] = down_first[places[F - 2 + k]]

    @pl.when(has_next)
    def _():
        tail_copy(1).start()
        tail_copy(2).start()

    def place(f):
        for source, base in ((first, 2), (up_first, 0), (down_first, 4)):
            block = source[places[f]]
            for line in range(2):
                value = spread(block[line * PACK : (line + 1) * PACK])
                grid_one[(2 if f < SPAN else 4) + f, base + line] = value
                if f in (2, 3):
                    grid_one[4 + f, base + line] = jnp.where(opened[1], jnp.zeros_like(value), value)

    line_of = lax.broadcasted_iota(jnp.int32, (2 * 4 * COLS, 1), 0) // COLS % 4
    outside = jnp.logical_or(
        jnp.logical_and(line_of == 0, jnp.logical_not(has_up)),
        jnp.logical_and(line_of == 3, jnp.logical_not(has_down)),
    )

    def second_of(base):
        hidden = conv(grid_one, base, 2, 4, w_one) + bias_one[...]
        mean = jnp.sum(hidden * hidden, axis=-1, keepdims=True) * (1.0 / CH)
        second = silu(hidden * lax.rsqrt(mean + 1e-06) * gain_two[...])
        second = jnp.where(outside, 0.0, second).astype(BF16).reshape(2, 4, COLS, CH)
        grid_two[base + 2 : base + 4] = second
        return second

    def finish(span):
        branch = conv(grid_two, 6 * span, SPAN, 2, w_two) + bias_two[...]
        for f in range(SPAN):
            block = arrived[places[SPAN * span + f]]
            for line in range(2):
                held = spread(block[line * PACK : (line + 1) * PACK]).astype(F32)
                at = (2 * f + line) * COLS
                out[SPAN * span + f, line] = (held + branch[at : at + COLS]).astype(BF16)

    for f in (4, 5, 6, 7):
        place(f)
    loads[1].wait()
    second = second_of(8)
    for k in range(2):
        for line in range(4):
            second_tail[k, line * PACK : (line + 1) * PACK] = gathered(second[k, line])
    send_second = remote(second_tail, second_before, s_send, s_recv, me + 1, row)

    @pl.when(has_next)
    def _():
        send_second.start()

    for f in (2, 3):
        place(f)
    second_of(6)
    for f in (0, 1):
        place(f)
    second = second_of(2)
    grid_two[6:8] = jnp.where(opened[1], jnp.zeros_like(second), second)
    loads[2].wait()
    finish(1)

    @pl.when(has_before)
    def _():
        for side in range(3):
            tail_copy(side).wait_recv()

    for side, base in ((0, 2), (1, 0), (2, 4)):
        for k in range(2):
            for line in range(2):
                value = spread(tail_before[side, k, line * PACK : (line + 1) * PACK])
                grid_one[k, base + line] = jnp.where(opened[0], jnp.zeros_like(value), value)
    second_of(0)

    @pl.when(has_before)
    def _():
        send_second.wait_recv()

    for k in range(2):
        for line in range(4):
            value = spread(second_before[k, line * PACK : (line + 1) * PACK])
            grid_two[k, line] = jnp.where(opened[0], jnp.zeros_like(value), value)
    finish(0)

    for step in ORDER:
        label_copies[step].wait_send()
        frame_copies[step].wait_send()
    for has_side, copies in ((has_up, up_near), (has_down, down_near)):

        @pl.when(has_side)
        def _():
            for step in (0,) + ORDER:
                copies[step].wait_send()

    @pl.when(has_next)
    def _():
        for side in range(3):
            tail_copy(side).wait_send()
        send_second.wait_send()


def body(
    frames_in, slot_frame, shot_spans, gain_one, conv_one, bias_one, gain_two, conv_two, bias_two
):
    vmem, smem, dma = pltpu.VMEM, pltpu.SMEM, pltpu.SemaphoreType.DMA
    whole = pl.BlockSpec(memory_space=vmem)
    hbm, scalars = pl.BlockSpec(memory_space=pl.ANY), pl.BlockSpec(memory_space=smem)
    taps, vector = (27, CH, CH), (1, CH)
    blocks = vmem((2 * N_TM, 2 * PACK, 128), BF16)
    return pl.pallas_call(
        functools.partial(kernel, lax.axis_size("rows")),
        out_shape=jax.ShapeDtypeStruct(frames_in.shape, BF16),
        in_specs=[hbm, scalars, scalars, whole, hbm, whole, whole, hbm, whole],
        out_specs=whole,
        scratch_shapes=[
            vmem(frames_in.shape, BF16),
            vmem(taps, BF16),
            vmem(taps, BF16),
            vmem((F, 2 * PACK, 128), BF16),
            vmem((F, 2 * PACK, 128), BF16),
            blocks, blocks, blocks, blocks, blocks, blocks,
            vmem((N_TM, 128), jnp.int32),
            smem((N_TM, 128), jnp.int32),
            vmem((3, 2, 2 * PACK, 128), BF16),
            vmem((3, 2, 2 * PACK, 128), BF16),
            vmem((2, 4 * PACK, 128), BF16),
            vmem((2, 4 * PACK, 128), BF16),
            vmem((12, 6, COLS, CH), BF16),
            vmem((12, 4, COLS, CH), BF16),
            dma((3,)),
            dma,
            dma((N_TM,)), dma((N_TM,)),
            dma((N_TM,)), dma((N_TM,)),
            dma((N_TM,)), dma((N_TM,)),
            dma((N_TM,)), dma((N_TM,)),
            dma((3,)), dma((3,)),
            dma, dma,
        ],
        name="residual_block",
        compiler_params=pltpu.CompilerParams(
            collective_id=1, has_side_effects=True, vmem_limit_bytes=60 << 20
        ),
    )(
        frames_in, slot_frame, shot_spans, gain_one.reshape(vector),
        conv_one.reshape(taps), bias_one.reshape(vector), gain_two.reshape(vector),
        conv_two.reshape(taps), bias_two.reshape(vector),
    )


def solution(mesh):
    placed = (P("tm", "rows", None, None), P("tm"), P(), P(), P(), P(), P(), P(), P())
    return jax.shard_map(
        body, mesh=mesh, in_specs=placed, out_specs=P("tm", "rows", None, None), check_vma=False
    )
```

time: 71.4 us -> 63.5 us (0.89)
  the two profiles are of different devices: /device:TPU:63 before, /device:TPU:448 now
where the time goes in v2:
time: 63.5 us; the launch traced here: 63.4 us
  Pallas kernels  61.7 us (97%)
  local copies, waits for them, and re-layouts  1.67 us (3%)
    pallas_call x1, Pallas kernels, body(): pl.pallas_call(functools.partial(kernel, lax.axis_size('rows')), out_shap...  61.7 us
    unnamed x1, local copies, waits for them, and re-layouts  1.67 us

profile of v2, /device:TPU:448, one launch (start us, length us, event | category | flops | bytes accessed | tf_op | source)
XLA Modules:
  0.0 63.4 jit_solution(6010930160618987593)
XLA Ops:
  0.0 61.7 %residual_block.1 = bf16[8,2,32,192]{3,2,1,0:T(8,128)(2,1)} custom-call(bf16[8,2,32,192]{3,2,1,0:T(8,128)(2,1)} %frames_h.1, s32[8]{0:T(128)} %slots.1, s32[4]{0:T(128)} %spans.1, f32[1,192]{1,0:T(1,128)} %bitcast.8, bf16[27,192,192]{2,1,0:T(8,128)(2,1)} %bitcast.6, f32[1,192]{1,0:T(1,128)} %bitcast.9, f32[1,192]{1,0:T(1,128)} %bitcast.10, ...), custom_call_target="tpu_custom_call" | custom-call | tf_op jit(solution)/shard_map/residual_block/pallas_call | solution.py:386
  61.7 1.7 %copy.11 = bf16[8,2,32,192]{3,2,1,0:T(8,128)(2,1)} copy(bf16[8,2,32,192]{3,2,1,0:T(8,128)(2,1)} %residual_block.1) | data formatting | bytes 393216

commit v3 on v2

--- a/solution.py
+++ b/solution.py
@@ -90,7 +90,7 @@
     row = lax.axis_index("rows")
     has_up, has_down = row > 0, row < n_rows - 1
     has_next, has_before = me < N_TM - 1, me > 0
-    far_up, far_down = row == n_rows, row == n_rows
+    far_up, far_down = row == n_rows // 2, row == n_rows // 2 - 1
     near_up = jnp.logical_and(has_up, jnp.logical_not(far_up))
     near_down = jnp.logical_and(has_down, jnp.logical_not(far_down))
 
@@ -116,8 +116,10 @@
 
         @pl.when(far)
         def _():
-            for tm in range(N_TM):
-                pl.semaphore_signal(barrier, inc=1, device_id=(tm, row + row_step), device_id_type=MESH)
+            for step in range(N_TM):
+                pl.semaphore_signal(
+                    barrier, inc=1, device_id=(lax.rem(me + step, N_TM), row + row_step), device_id_type=MESH
+                )
 
     lane = lax.broadcasted_iota(jnp.int32, (1, 128), 1)
     held = jnp.zeros((1, 128), jnp.int32)

time: 63.5 us -> 52.3 us (0.82)
  the two profiles are of different devices: /device:TPU:448 before, /device:TPU:159 now
where the time goes in v3:
time: 52.3 us; the launch traced here: 52.2 us
  Pallas kernels  50.5 us (97%)
  local copies, waits for them, and re-layouts  1.67 us (3%)
    pallas_call x1, Pallas kernels, body(): pl.pallas_call(functools.partial(kernel, lax.axis_size('rows')), out_shap...  50.5 us
    unnamed x1, local copies, waits for them, and re-layouts  1.67 us

profile of v3, /device:TPU:159, one launch (start us, length us, event | category | flops | bytes accessed | tf_op | source)
XLA Modules:
  0.0 52.2 jit_solution(7596317405958817416)
XLA Ops:
  0.0 50.5 %residual_block.1 = bf16[8,2,32,192]{3,2,1,0:T(8,128)(2,1)} custom-call(bf16[8,2,32,192]{3,2,1,0:T(8,128)(2,1)} %frames_h.1, s32[8]{0:T(128)} %slots.1, s32[4]{0:T(128)} %spans.1, f32[1,192]{1,0:T(1,128)} %bitcast.8, bf16[27,192,192]{2,1,0:T(8,128)(2,1)} %bitcast.6, f32[1,192]{1,0:T(1,128)} %bitcast.9, f32[1,192]{1,0:T(1,128)} %bitcast.10, ...), custom_call_target="tpu_custom_call" | custom-call | tf_op jit(solution)/shard_map/residual_block/pallas_call | solution.py:388
  50.5 1.7 %copy.11 = bf16[8,2,32,192]{3,2,1,0:T(8,128)(2,1)} copy(bf16[8,2,32,192]{3,2,1,0:T(8,128)(2,1)} %residual_block.1) | data formatting | bytes 393216

commit v4 on v3

--- a/solution.py
+++ b/solution.py
@@ -13,7 +13,8 @@
 N_TM = 8
 F = 8
 PACK = 48
-ORDER = (4, 3, 5, 2, 6, 1, 7)
+ORDER = (1, 7, 2, 6, 3, 5, 4)
+WINDOW = 4
 F32 = jnp.float32
 BF16 = jnp.bfloat16
 MESH = pl.DeviceIdType.MESH
@@ -64,12 +65,13 @@
     return middle + from_left + from_right
 
 
-def conv(source, base, frames, rows, weight):
+def conv(source, base, frames, rows, weight, time_taps):
     count = frames * rows * COLS
     sums = [jnp.zeros((count, CH), F32) for _ in range(3)]
-    for time_tap in range(3):
+    for time_tap in time_taps:
+        at = base if len(time_taps) == 1 else base + time_tap
         for row_tap in range(3):
-            tile = source[pl.ds(base + time_tap, frames), pl.ds(row_tap, rows)].reshape(count, CH)
+            tile = source[pl.ds(at, frames), pl.ds(row_tap, rows)].reshape(count, CH)
             for col_tap in range(3):
                 tap = weight[(time_tap * 3 + row_tap) * 3 + col_tap]
                 sums[col_tap] = sums[col_tap] + jnp.dot(tile, tap, preferred_element_type=F32)
@@ -78,48 +80,52 @@
 
 def kernel(
     n_rows,
-    frames_h, slots, spans, gain_one, conv_one_h, bias_one, gain_two, conv_two_h, bias_two,
+    frames_h, slots, spans, gain_one_h, conv_one_h, bias_one_h, gain_two_h, conv_two_h, bias_two_h,
     out,
-    frames, w_one, w_two,
+    frames, gain_one, w_one, bias_one, gain_two, w_two, bias_two,
     packed, packed_first, outgoing, outgoing_first, arrived, first, up_first, down_first,
-    labels, labels_s, tail, tail_before, second_tail, second_before, grid_one, grid_two,
+    labels, labels_s, tail, tail_before, second_tail, second_before, grid_one, grid_tail, parts, grid_two,
     in_sem, label_sem, l_send, l_recv, a_send, a_recv, up_send, up_recv, down_send, down_recv,
-    t_send, t_recv, s_send, s_recv,
+    t_send, t_recv, s_send, s_recv, gate_sem, line_sem,
 ):
     me = lax.axis_index("tm")
     row = lax.axis_index("rows")
     has_up, has_down = row > 0, row < n_rows - 1
     has_next, has_before = me < N_TM - 1, me > 0
     far_up, far_down = row == n_rows // 2, row == n_rows // 2 - 1
+    far = jnp.logical_or(far_up, far_down)
+    ends = jnp.logical_or(me == 0, me == N_TM - 1)
     near_up = jnp.logical_and(has_up, jnp.logical_not(far_up))
     near_down = jnp.logical_and(has_down, jnp.logical_not(far_down))
+
+    barrier = pltpu.get_barrier_semaphore()
+    peers = jnp.int32(N_TM - 1)
+    for near, across, row_step in ((near_up, far_up, -1), (near_down, far_down, 1)):
+        greets = jnp.logical_and(across, ends)
+        peers = peers + near.astype(jnp.int32) + greets.astype(jnp.int32)
+
+        @pl.when(near)
+        def _():
+            pl.semaphore_signal(barrier, inc=1, device_id=(me, row + row_step), device_id_type=MESH)
+
+        @pl.when(greets)
+        def _():
+            pl.semaphore_signal(
+                barrier, inc=1, device_id=(N_TM - 1 - me, row + row_step), device_id_type=MESH
+            )
+
+    for step in ORDER:
+        pl.semaphore_signal(barrier, inc=1, device_id=(lax.rem(me + step, N_TM), row), device_id_type=MESH)
 
     loads = [
         pltpu.make_async_copy(src, dst, in_sem.at[i])
         for i, (src, dst) in enumerate((
-            (frames_h, frames), (conv_one_h, w_one), (conv_two_h, w_two),
+            (frames_h, frames), (gain_one_h, gain_one), (bias_one_h, bias_one), (gain_two_h, gain_two),
+            (bias_two_h, bias_two), (conv_one_h, w_one), (conv_two_h, w_two),
         ))
     ]
     for load in loads:
         load.start()
-
-    barrier = pltpu.get_barrier_semaphore()
-    for step in range(1, N_TM):
-        pl.semaphore_signal(barrier, inc=1, device_id=(lax.rem(me + step, N_TM), row), device_id_type=MESH)
-    peers = jnp.int32(N_TM - 1)
-    for near, far, row_step in ((near_up, far_up, -1), (near_down, far_down, 1)):
-        peers = peers + near.astype(jnp.int32) + N_TM * far.astype(jnp.int32)
-
-        @pl.when(near)
-        def _():
-            pl.semaphore_signal(barrier, inc=1, device_id=(me, row + row_step), device_id_type=MESH)
-
-        @pl.when(far)
-        def _():
-            for step in range(N_TM):
-                pl.semaphore_signal(
-                    barrier, inc=1, device_id=(lax.rem(me + step, N_TM), row + row_step), device_id_type=MESH
-                )
 
     lane = lax.broadcasted_iota(jnp.int32, (1, 128), 1)
     held = jnp.zeros((1, 128), jnp.int32)
@@ -128,6 +134,7 @@
     labels[0:1] = held
 
     loads[0].wait()
+    loads[1].wait()
     gain = gain_one[...]
     gain_low = gain[:, :128]
     gain_pairs = jnp.concatenate([gain[:, 128:], gain[:, 128:]], axis=1)
@@ -196,14 +203,24 @@
 
     for step in ORDER:
         label_copies[step].start()
-    for step in ORDER:
+    order = (0,) + ORDER
+    for step in order[1 : WINDOW + 1]:
         frame_copies[step].start()
-    for far, copies in ((far_up, up_far), (far_down, down_far)):
-
-        @pl.when(far)
+
+    for across, row_step in ((far_up, -1), (far_down, 1)):
+
+        @pl.when(jnp.logical_and(across, ends))
         def _():
-            for step in ORDER + (0,):
-                copies[step].start()
+            pl.semaphore_signal(
+                gate_sem, inc=1, device_id=(N_TM - 1 - me, row + row_step), device_id_type=MESH
+            )
+
+    @pl.when(jnp.logical_and(far, ends))
+    def _():
+        pl.semaphore_wait(gate_sem, 1)
+        for distance in range(1, N_TM // 2):
+            target = jnp.where(me == 0, me + distance, me - distance)
+            pl.semaphore_signal(line_sem, inc=1, device_id=(target, row), device_id_type=MESH)
 
     forward(0)
 
@@ -219,25 +236,6 @@
     def _():
         tail_before[...] = jnp.zeros_like(tail_before)
         second_before[...] = jnp.zeros_like(second_before)
-
-    for step in ORDER:
-        label_copies[step].wait_recv()
-    to_scalars = pltpu.make_async_copy(labels, labels_s, label_sem)
-    to_scalars.start()
-    to_scalars.wait()
-
-    def scan_source(step, places):
-        count = jnp.int32(0)
-        for slot in range(F):
-            held = labels_s[step, slot]
-            mine = lax.shift_right_logical(held, 3) == me
-            local = jnp.bitwise_and(held, F - 1)
-            at = 2 * step + jnp.minimum(count, 1)
-            places = tuple(jnp.where(jnp.logical_and(mine, local == f), at, places[f]) for f in range(F))
-            count = count + mine.astype(jnp.int32)
-        return places
-
-    places = lax.fori_loop(0, N_TM, scan_source, (jnp.int32(0),) * F)
 
     opened = []
     for span in range(2):
@@ -247,7 +245,27 @@
             start = start + spans[shot]
         opened.append(hit)
 
-    for step in ORDER:
+    def find_places():
+        for step in ORDER:
+            label_copies[step].wait_recv()
+        to_scalars = pltpu.make_async_copy(labels, labels_s, label_sem)
+        to_scalars.start()
+        to_scalars.wait()
+
+        def scan_source(step, places):
+            count = jnp.int32(0)
+            for slot in range(F):
+                held = labels_s[step, slot]
+                mine = lax.shift_right_logical(held, 3) == me
+                local = jnp.bitwise_and(held, F - 1)
+                at = 2 * step + jnp.minimum(count, 1)
+                places = tuple(jnp.where(jnp.logical_and(mine, local == f), at, places[f]) for f in range(F))
+                count = count + mine.astype(jnp.int32)
+            return places
+
+        return lax.fori_loop(0, N_TM, scan_source, (jnp.int32(0),) * F)
+
+    def take_in(step):
         frame_copies[step].wait_recv()
         for rank in range(2):
             for line in range(2):
@@ -257,6 +275,57 @@
                 )
         forward(step)
 
+    def wait_halo(step):
+        for has_side, copies in ((has_down, up_near), (has_up, down_near)):
+
+            @pl.when(has_side)
+            def _():
+                copies[step].wait_recv()
+
+    def convolve_pair(at, slots_of):
+        for k in range(2):
+            for source, base in ((first, 2), (up_first, 0), (down_first, 4)):
+                block = source[slots_of[k]]
+                for line in range(2):
+                    grid_one[at + k, base + line] = spread(block[line * PACK : (line + 1) * PACK])
+        for time_tap in range(3):
+            share = conv(grid_one, at, 2, 4, w_one, (time_tap,))
+            parts[time_tap, at : at + 2] = share.reshape(2, 4, COLS, CH)
+
+    def convolve(step):
+        convolve_pair(2 * step, (2 * step, 2 * step + 1))
+
+    def convolve_video(f):
+        convolve_pair(f, places[f : f + 2])
+
+    for i in range(1, N_TM):
+        take_in(order[i])
+        if i + WINDOW < N_TM:
+            frame_copies[order[i]].wait_send()
+            frame_copies[order[i + WINDOW]].start()
+        if i == 1:
+
+            @pl.when(jnp.logical_and(far, jnp.logical_not(ends)))
+            def _():
+                pl.semaphore_wait(line_sem, 1)
+
+            for across, copies in ((far_up, up_far), (far_down, down_far)):
+
+                @pl.when(across)
+                def _():
+                    for step in order:
+                        copies[step].start()
+
+        if i == 2:
+            loads[5].wait()
+            places = find_places()
+        if i >= 2:
+
+            @pl.when(jnp.logical_not(far))
+            def _():
+                wait_halo(order[i - 2])
+                convolve(order[i - 2])
+
     def tail_copy(side):
         return remote(tail.at[side], tail_before.at[side], t_send.at[side], t_recv.at[side], me + 1, row)
 
@@ -267,12 +336,16 @@
     def _():
         tail_copy(0).start()
 
-    for has_side, copies in ((has_down, up_near), (has_up, down_near)):
-
-        @pl.when(has_side)
-        def _():
-            for step in (0,) + ORDER:
-                copies[step].wait_recv()
+    @pl.when(jnp.logical_not(far))
+    def _():
+        wait_halo(order[-2])
+        convolve(order[-2])
+        wait_halo(order[-1])
+
+    @pl.when(far)
+    def _():
+        for step in order:
+            wait_halo(step)
 
     for k in range(2):
         tail[1, k] = up_first[places[F - 2 + k]]
@@ -283,14 +356,18 @@
         tail_copy(1).start()
         tail_copy(2).start()
 
-    def place(f):
-        for source, base in ((first, 2), (up_first, 0), (down_first, 4)):
-            block = source[places[f]]
-            for line in range(2):
-                value = spread(block[line * PACK : (line + 1) * PACK])
-                grid_one[(2 if f < SPAN else 4) + f, base + line] = value
-                if f in (2, 3):
-                    grid_one[4 + f, base + line] = jnp.where(opened[1], jnp.zeros_like(value), value)
+    @pl.when(jnp.logical_not(far))
+    def _():
+        convolve(order[-1])
+
+    @pl.when(far)
+    def _():
+        convolve_video(6)
+        convolve_video(4)
+
+    spots = [jnp.where(far, f, places[f]) for f in range(F)]
+    for load in loads[2:5]:
+        load.wait()
 
     line_of = lax.broadcasted_iota(jnp.int32, (2 * 4 * COLS, 1), 0) // COLS % 4
     outside = jnp.logical_or(
@@ -298,16 +375,25 @@
         jnp.logical_and(line_of == 3, jnp.logical_not(has_down)),
     )
 
-    def second_of(base):
-        hidden = conv(grid_one, base, 2, 4, w_one) + bias_one[...]
+    def part(time_tap, f):
+        return parts[time_tap, spots[f]].reshape(4 * COLS, CH)
+
+    def cut(span, share):
+        return jnp.where(opened[span], jnp.zeros_like(share), share)
+
+    def second_of(at, hidden):
+        hidden = jnp.concatenate(hidden, axis=0) + bias_one[...]
         mean = jnp.sum(hidden * hidden, axis=-1, keepdims=True) * (1.0 / CH)
         second = silu(hidden * lax.rsqrt(mean + 1e-06) * gain_two[...])
         second = jnp.where(outside, 0.0, second).astype(BF16).reshape(2, 4, COLS, CH)
-        grid_two[base + 2 : base + 4] = second
+        grid_two[at : at + 2] = second
         return second
 
+    def whole(f):
+        return part(2, f) + part(1, f - 1) + part(0, f - 2)
+
     def finish(span):
-        branch = conv(grid_two, 6 * span, SPAN, 2, w_two) + bias_two[...]
+        branch = conv(grid_two, 6 * span, SPAN, 2, w_two, (0, 1, 2)) + bias_two[...]
         for f in range(SPAN):
             block = arrived[places[SPAN * span + f]]
             for line in range(2):
@@ -315,10 +401,7 @@
                 at = (2 * f + line) * COLS
                 out[SPAN * span + f, line] = (held + branch[at : at + COLS]).astype(BF16)
 
-    for f in (4, 5, 6, 7):
-        place(f)
-    loads[1].wait()
-    second = second_of(8)
+    second = second_of(10, [whole(6), whole(7)])
     for k in range(2):
         for line in range(4):
             second_tail[k, line * PACK : (line + 1) * PACK] = gathered(second[k, line])
@@ -328,14 +411,18 @@
     def _():
         send_second.start()
 
-    for f in (2, 3):
-        place(f)
-    second_of(6)
-    for f in (0, 1):
-        place(f)
-    second = second_of(2)
+    @pl.when(far)
+    def _():
+        convolve_video(2)
+        convolve_video(0)
+
+    second_of(8, [
+        part(2, 4) + cut(1, part(1, 3) + part(0, 2)),
+        part(2, 5) + part(1, 4) + cut(1, part(0, 3)),
+    ])
+    second = second_of(4, [whole(2), whole(3)])
     grid_two[6:8] = jnp.where(opened[1], jnp.zeros_like(second), second)
-    loads[2].wait()
+    loads[6].wait()
     finish(1)
 
     @pl.when(has_before)
@@ -346,9 +433,13 @@
     for side, base in ((0, 2), (1, 0), (2, 4)):
         for k in range(2):
             for line in range(2):
-                value = spread(tail_before[side, k, line * PACK : (line + 1) * PACK])
-                grid_one[k, base + line] = jnp.where(opened[0], jnp.zeros_like(value), value)
-    second_of(0)
+                grid_tail[k, base + line] = spread(tail_before[side, k, line * PACK : (line + 1) * PACK])
+    two_back = conv(grid_tail, 0, 2, 4, w_one, (0,))
+    one_back = conv(grid_tail, 1, 1, 4, w_one, (1,))
+    second_of(2, [
+        part(2, 0) + cut(0, one_back + two_back[: 4 * COLS]),
+        part(2, 1) + part(1, 0) + cut(0, two_back[4 * COLS :]),
+    ])
 
     @pl.when(has_before)
     def _():
@@ -362,12 +453,13 @@
 
     for step in ORDER:
         label_copies[step].wait_send()
+    for step in order[N_TM - WINDOW :]:
         frame_copies[step].wait_send()
     for has_side, copies in ((has_up, up_near), (has_down, down_near)):
 
         @pl.when(has_side)
         def _():
-            for step in (0,) + ORDER:
+            for step in order:
                 copies[step].wait_send()
 
     @pl.when(has_next)
@@ -382,18 +474,22 @@
 ):
     vmem, smem, dma = pltpu.VMEM, pltpu.SMEM, pltpu.SemaphoreType.DMA
     whole = pl.BlockSpec(memory_space=vmem)
-    hbm, scalars = pl.BlockSpec(memory_space=pl.ANY), pl.BlockSpec(memory_space=smem)
+    hbm, scalars = pl.BlockSpec(memory_space=pltpu.HBM), pl.BlockSpec(memory_space=smem)
     taps, vector = (27, CH, CH), (1, CH)
     blocks = vmem((2 * N_TM, 2 * PACK, 128), BF16)
     return pl.pallas_call(
         functools.partial(kernel, lax.axis_size("rows")),
         out_shape=jax.ShapeDtypeStruct(frames_in.shape, BF16),
-        in_specs=[hbm, scalars, scalars, whole, hbm, whole, whole, hbm, whole],
+        in_specs=[hbm, scalars, scalars] + [hbm] * 6,
         out_specs=whole,
         scratch_shapes=[
             vmem(frames_in.shape, BF16),
+            vmem(vector, F32),
             vmem(taps, BF16),
+            vmem(vector, F32),
+            vmem(vector, F32),
             vmem(taps, BF16),
+            vmem(vector, F32),
             vmem((F, 2 * PACK, 128), BF16),
             vmem((F, 2 * PACK, 128), BF16),
             blocks, blocks, blocks, blocks, blocks, blocks,
@@ -403,9 +499,11 @@
             vmem((3, 2, 2 * PACK, 128), BF16),
             vmem((2, 4 * PACK, 128), BF16),
             vmem((2, 4 * PACK, 128), BF16),
-            vmem((12, 6, COLS, CH), BF16),
+            vmem((2 * N_TM, 6, COLS, CH), BF16),
+            vmem((2, 6, COLS, CH), BF16),
+            vmem((3, 2 * N_TM, 4, COLS, CH), F32),
             vmem((12, 4, COLS, CH), BF16),
-            dma((3,)),
+            dma((7,)),
             dma,
             dma((N_TM,)), dma((N_TM,)),
             dma((N_TM,)), dma((N_TM,)),
@@ -413,6 +511,7 @@
             dma((N_TM,)), dma((N_TM,)),
             dma((3,)), dma((3,)),
             dma, dma,
+            pltpu.SemaphoreType.REGULAR, pltpu.SemaphoreType.REGULAR,
         ],
         name="residual_block",
         compiler_params=pltpu.CompilerParams(

time: 52.3 us -> 51.7 us (0.989)
  the two profiles are of different devices: /device:TPU:159 before, /device:TPU:31 now
where the time goes in v4:
time: 51.7 us; the launch traced here: 51.5 us
  Pallas kernels  49.8 us (96%)
  local copies, waits for them, and re-layouts  1.67 us (3%)
    pallas_call x1, Pallas kernels, body(): pl.pallas_call(functools.partial(kernel, lax.axis_size('rows')), out_shap...  49.8 us
    unnamed x1, local copies, waits for them, and re-layouts  1.67 us

profile of v4, /device:TPU:31, one launch (start us, length us, event | category | flops | bytes accessed | tf_op | source)
XLA Modules:
  0.0 51.5 jit_solution(10450457131291158424)
XLA Ops:
  0.0 49.8 %residual_block.1 = bf16[8,2,32,192]{3,2,1,0:T(8,128)(2,1)} custom-call(bf16[8,2,32,192]{3,2,1,0:T(8,128)(2,1)} %frames_h.1, s32[8]{0:T(128)} %slots.1, s32[4]{0:T(128)} %spans.1, f32[1,192]{1,0:T(1,128)} %bitcast.8, bf16[27,192,192]{2,1,0:T(8,128)(2,1)} %bitcast.6, f32[1,192]{1,0:T(1,128)} %bitcast.9, f32[1,192]{1,0:T(1,128)} %bitcast.10, ...), custom_call_target="tpu_custom_call" | custom-call | tf_op jit(solution)/shard_map/residual_block/pallas_call | solution.py:480
  49.8 1.7 %copy.11 = bf16[8,2,32,192]{3,2,1,0:T(8,128)(2,1)} copy(bf16[8,2,32,192]{3,2,1,0:T(8,128)(2,1)} %residual_block.1) | data formatting | bytes 393216

commit v5 on v4

--- a/solution.py
+++ b/solution.py
@@ -65,13 +65,13 @@
     return middle + from_left + from_right
 
 
-def conv(source, base, frames, rows, weight, time_taps):
+def conv(source, base, frames, rows, weight, time_taps, first_row=0):
     count = frames * rows * COLS
     sums = [jnp.zeros((count, CH), F32) for _ in range(3)]
     for time_tap in time_taps:
         at = base if len(time_taps) == 1 else base + time_tap
         for row_tap in range(3):
-            tile = source[pl.ds(at, frames), pl.ds(row_tap, rows)].reshape(count, CH)
+            tile = source[pl.ds(at, frames), pl.ds(first_row + row_tap, rows)].reshape(count, CH)
             for col_tap in range(3):
                 tap = weight[(time_tap * 3 + row_tap) * 3 + col_tap]
                 sums[col_tap] = sums[col_tap] + jnp.dot(tile, tap, preferred_element_type=F32)
@@ -295,8 +295,25 @@
     def convolve(step):
         convolve_pair(2 * step, (2 * step, 2 * step + 1))
 
-    def convolve_video(f):
-        convolve_pair(f, places[f : f + 2])
+    def lay_video(source, base):
+        for f in range(F):
+            block = source[places[f]]
+            for line in range(2):
+                grid_one[f, base + line] = spread(block[line * PACK : (line + 1) * PACK])
+
+    def convolve_half(f, first_row):
+        for time_tap in range(3):
+            share = conv(grid_one, f, SPAN, 2, w_one, (time_tap,), first_row)
+            parts[time_tap, f : f + SPAN, pl.ds(first_row, 2)] = share.reshape(SPAN, 2, COLS, CH)
+
+    def wait_all(there, copies):
+        @pl.when(there)
+        def _():
+            for step in order:
+                copies[step].wait_recv()
+
+    near_rows = jnp.where(far_down, 0, 2)
+    far_rows = 2 - near_rows
 
     for i in range(1, N_TM):
         take_in(order[i])
@@ -344,8 +361,17 @@
 
     @pl.when(far)
     def _():
-        for step in order:
-            wait_halo(step)
+        lay_video(first, 2)
+        wait_all(jnp.logical_and(far_down, has_up), down_near)
+        wait_all(jnp.logical_and(far_up, has_down), up_near)
+        pl.when(far_down)(functools.partial(lay_video, up_first, 0))
+        pl.when(far_up)(functools.partial(lay_video, down_first, 4))
+        convolve_half(SPAN, near_rows)
+        convolve_half(0, near_rows)
+        wait_all(far_down, up_near)
+        wait_all(far_up, down_near)
+        pl.when(far_down)(functools.partial(lay_video, down_first, 4))
+        pl.when(far_up)(functools.partial(lay_video, up_first, 0))
 
     for k in range(2):
         tail[1, k] = up_first[places[F - 2 + k]]
@@ -362,8 +388,7 @@
 
     @pl.when(far)
     def _():
-        convolve_video(6)
-        convolve_video(4)
+        convolve_half(SPAN, far_rows)
 
     spots = [jnp.where(far, f, places[f]) for f in range(F)]
     for load in loads[2:5]:
@@ -413,8 +438,7 @@
 
     @pl.when(far)
     def _():
-        convolve_video(2)
-        convolve_video(0)
+        convolve_half(0, far_rows)
 
     second_of(8, [
         part(2, 4) + cut(1, part(1, 3) + part(0, 2)),

time: 51.7 us -> 49.9 us (0.965)
  Pallas kernels: 49.8 us -> 48.1 us
    pallas_call x1, Pallas kernels: 49.8 us -> 48.1 us  [body(): pl.pallas_call(functools.partial(kernel, lax.axis_size('rows')), out_shap...]
where the time goes in v5:
time: 49.9 us; the launch traced here: 49.8 us
  Pallas kernels  48.1 us (96%)
  local copies, waits for them, and re-layouts  1.67 us (3%)
    pallas_call x1, Pallas kernels, body(): pl.pallas_call(functools.partial(kernel, lax.axis_size('rows')), out_shap...  48.1 us
    unnamed x1, local copies, waits for them, and re-layouts  1.67 us

profile of v5, /device:TPU:31, one launch (start us, length us, event | category | flops | bytes accessed | tf_op | source)
XLA Modules:
  0.0 49.8 jit_solution(15511053719762419211)
XLA Ops:
  0.0 48.1 %residual_block.1 = bf16[8,2,32,192]{3,2,1,0:T(8,128)(2,1)} custom-call(bf16[8,2,32,192]{3,2,1,0:T(8,128)(2,1)} %frames_h.1, s32[8]{0:T(128)} %slots.1, s32[4]{0:T(128)} %spans.1, f32[1,192]{1,0:T(1,128)} %bitcast.8, bf16[27,192,192]{2,1,0:T(8,128)(2,1)} %bitcast.6, f32[1,192]{1,0:T(1,128)} %bitcast.9, f32[1,192]{1,0:T(1,128)} %bitcast.10, ...), custom_call_target="tpu_custom_call" | custom-call | tf_op jit(solution)/shard_map/residual_block/pallas_call | solution.py:504
  48.1 1.7 %copy.11 = bf16[8,2,32,192]{3,2,1,0:T(8,128)(2,1)} copy(bf16[8,2,32,192]{3,2,1,0:T(8,128)(2,1)} %residual_block.1) | data formatting | bytes 393216

commit v6 on v5

--- a/solution.py
+++ b/solution.py
@@ -14,7 +14,7 @@
 F = 8
 PACK = 48
 ORDER = (1, 7, 2, 6, 3, 5, 4)
-WINDOW = 4
+WINDOW = 5
 F32 = jnp.float32
 BF16 = jnp.bfloat16
 MESH = pl.DeviceIdType.MESH

time: 49.9 us -> 49.3 us (0.988)
  Pallas kernels: 48.1 us -> 47.5 us
    pallas_call x1, Pallas kernels: 48.1 us -> 47.5 us  [body(): pl.pallas_call(functools.partial(kernel, lax.axis_size('rows')), out_shap...]
where the time goes in v6:
time: 49.3 us; the launch traced here: 49.1 us
  Pallas kernels  47.5 us (96%)
  local copies, waits for them, and re-layouts  1.67 us (3%)
    pallas_call x1, Pallas kernels, body(): pl.pallas_call(functools.partial(kernel, lax.axis_size('rows')), out_shap...  47.5 us
    unnamed x1, local copies, waits for them, and re-layouts  1.67 us

profile of v6, /device:TPU:31, one launch (start us, length us, event | category | flops | bytes accessed | tf_op | source)
XLA Modules:
  0.0 49.1 jit_solution(9480516473857561795)
XLA Ops:
  0.0 47.5 %residual_block.1 = bf16[8,2,32,192]{3,2,1,0:T(8,128)(2,1)} custom-call(bf16[8,2,32,192]{3,2,1,0:T(8,128)(2,1)} %frames_h.1, s32[8]{0:T(128)} %slots.1, s32[4]{0:T(128)} %spans.1, f32[1,192]{1,0:T(1,128)} %bitcast.8, bf16[27,192,192]{2,1,0:T(8,128)(2,1)} %bitcast.6, f32[1,192]{1,0:T(1,128)} %bitcast.9, f32[1,192]{1,0:T(1,128)} %bitcast.10, ...), custom_call_target="tpu_custom_call" | custom-call | tf_op jit(solution)/shard_map/residual_block/pallas_call | solution.py:504
  47.5 1.7 %copy.11 = bf16[8,2,32,192]{3,2,1,0:T(8,128)(2,1)} copy(bf16[8,2,32,192]{3,2,1,0:T(8,128)(2,1)} %residual_block.1) | data formatting | bytes 393216
